TPU v7x, 32 devices: a whole 2x2x4 slice. The times are simulated.
32 devices in a mesh: row: 4 (over y, x), col: 8 (over z, core).
Axes of the slice: x: 2, y: 2, z: 4, core: 2. Of those that a mesh axis runs over, the one named last changes fastest.
Arguments:
- operator: float32 [24576, 24576], P('row', 'col'), may hold values from -0.0546875 to 0.0546875
- modes: float32 [16, 84, 24576], P(None, None, ('col', 'row')), may hold values from -6 to 6
- coupling: float32 [84, 84], replicated, may hold values from -0.625 to 0.625
Outputs:
- mixed: float32 [16, 84, 24576], P(None, None, ('row', 'col'))
All inputs are finite; a program needn't handle non-finite values.
Results may differ from a plain program's by a relative error of at most 0.000071.
Values sent between devices are 32-bit elements; how exact they have to be, the bound alone decides.
No kernel may reach another device: no remote copies, remote signals or barrier semaphores. Data moves between devices by JAX's collectives and lax.ppermute only.
A program may use at most 192 MiB of HBM per device.

v0:
```python
import jax
import jax.numpy as jnp
from jax import lax
from jax.sharding import PartitionSpec as P


def contract(left, right):
    return lax.dot_general(
        left,
        right,
        (((2,), (1,)), ((), ())),
        precision=lax.Precision.HIGHEST,
        preferred_element_type=jnp.float32,
    )


def mix_modes(coupling, summed):
    return jnp.einsum("pq,kqi->kpi", coupling, summed, precision=lax.Precision.HIGHEST)


def per_device(operator, modes, coupling):
    gathered = lax.all_gather(modes, "row", axis=2, tiled=True)
    summed = lax.psum_scatter(contract(gathered, operator), "col", scatter_dimension=2, tiled=True)
    return mix_modes(coupling, summed)


def solution(mesh):
    in_specs = (P("row", "col"), P(None, None, ("col", "row")), P())
    out_specs = P(None, None, ("row", "col"))
    return jax.shard_map(
        per_device, mesh=mesh, in_specs=in_specs, out_specs=out_specs, check_vma=False
    )
```

profile of v0, /device:TPU:0, one launch (start us, length us, event | category | flops | bytes accessed | tf_op | source)
XLA Modules:
  0.0 914.2 jit_solution(17769471575564550664)
XLA Ops:
  6.5 0.0 copy-start
  6.5 0.0 all-gather.2.cloned.1.call-start
  6.5 0.7 all-gather.2.cloned.1.call-update
  7.3 0.0 reduce-scatter.2.cloned.1.call-start
  7.3 159.9 %all-gather.2.cloned.1.call-done = f32[16,84,3072]{2,0,1:T(8,128)} async-done(((f32[16,84,768]{2,0,1:T(8,128)}), f32[16,84,3072]{2,0,1:T(8,128)}) %all-gather.2.cloned.1.call-update) | async-done | bytes 16515088 | tf_op jit(solution)/shard_map/all_gather | solution.py:22
  167.2 395.6 %fusion = f32[16,84,6144]{2,1,0:T(8,128)} fusion(f32[6144,3072]{1,0:T(8,128)} %param.3, f32[16,84,3072]{2,0,1:T(8,128)} %all-gather.2.cloned.1.call-done), kind=kOutput, calls=%fused_computation | convolution fusion | flops 304405807104 | bytes 125042688 | tf_op jit(solution)/shard_map/dot_general | solution.py:8
  562.7 0.0 reduce-scatter.2.cloned.1.call-update
  562.8 335.6 %reduce-scatter.2.cloned.1.call-done = f32[16,84,768]{2,1,0:T(8,128)} async-done(((f32[16,84,6144]{2,1,0:T(8,128)}), f32[16,84,768]{2,1,0:T(8,128)}) %reduce-scatter.2.cloned.1.call-update) | async-done | bytes 4128784 | tf_op jit(solution)/shard_map/reduce_scatter | solution.py:23
  898.3 0.0 copy-done
  898.4 5.7 convolution_bitcast_fusion
  904.1 3.2 copy.4
Async XLA Ops:
  6.5 891.8 %copy-start = (f32[84,84]{1,0:T(8,128)S(1)}, f32[84,84]{1,0:T(8,128)}, u32[]{:S(2)}) copy-start(f32[84,84]{1,0:T(8,128)} %param.5) | copy-start | bytes 84676
  6.5 160.6 %all-gather.2.cloned.1.call-start = ((), (), s32[]{:S(2)}) async-start(), calls=%async_computation.1 | async-start | bytes 20643840 | tf_op jit(solution)/shard_map/all_gather | solution.py:22
  7.3 891.1 %reduce-scatter.2.cloned.1.call-start = ((), (), s32[]{:S(2)}) async-start(), calls=%async_computation.2 | async-start | bytes 38928384 | tf_op jit(solution)/shard_map/reduce_scatter | solution.py:23
Sparse Core Ops, SparseCore 0:
  9.2 157.9 all-gather.1
  562.9 335.4 reduce-scatter.1
where the time goes:
time: 914 us
  waiting for transfers between devices  496 us (54%)
  matrix products  401 us (44%)
  between operations  13.4 us (1%)
    dot_general x1, matrix products, contract(): lax.dot_general(left, right, (((2,), (1,)), ((), ())), precision=lax.Prec...  396 us
    reduce_scatter x1, waiting for transfers between devices, per_device(): lax.psum_scatter(contract(gathered, operator), 'col', scatter_dimension=2...  336 us
    all_gather x1, waiting for transfers between devices, per_device(): gathered = lax.all_gather(modes, 'row', axis=2, tiled=True)  160 us
  transfers between devices with their start and end apart: 2, of which 2 were waited for; matrix products, arithmetic and copies ran while one was open for 0% of the time, Pallas kernels for 0%

commit v1 on v0

v1 whole, which is shorter than its diff:
```python
import functools

import jax
import jax.numpy as jnp
from jax import lax
from jax.experimental import pallas as pl
from jax.experimental.pallas import tpu as pltpu
from jax.sharding import PartitionSpec as P

CUTS = (0.131, 0.31, 0.607)
F32, BF16 = jnp.float32, jnp.bfloat16
LAST = (((1,), (1,)), ((), ()))
FIRST = (((1,), (0,)), ((), ()))
PARAMS = pltpu.CompilerParams(vmem_limit_bytes=64 * 2**20)
HBM = pl.BlockSpec(memory_space=pltpu.HBM)


def shares(count):
    cuts = [0] + [round(count * c) for c in CUTS] + [count]
    return [b - a for a, b in zip(cuts, cuts[1:])]


def halves(x):
    high = x.astype(BF16)
    return high, (x - high.astype(F32)).astype(BF16)


def dot(a, b, dims=LAST):
    return lax.dot_general(a, b, dims, preferred_element_type=F32)


def cost(products):
    return pl.CostEstimate(flops=6 * products, bytes_accessed=0, transcendentals=0)


def product_kernel(pieces, n_deps, where_ref, at_ref, *refs):
    parts, op_ref = refs[:pieces], refs[pieces]
    out_ref, split = refs[pieces + 1 + n_deps :]
    rows = parts[0].shape[1]

    @pl.when(pl.program_id(0) == 0)
    def _():
        for n, part in enumerate(parts):
            width = part.shape[2]
            for r in range(part.shape[0]):
                high, low = halves(part[r])
                start = r * width if pieces == 1 else pl.multiple_of(at_ref[n], 128)
                split[:rows, pl.ds(start, width)] = high
                split[rows:, pl.ds(start, width)] = low

    high, low = halves(op_ref[...])
    both = dot(split[...], high)
    out_ref[0] = both[:rows] + (both[rows:] + dot(split[:rows], low))


def product(parts, at, operator, width, where, deps=()):
    nb, rows, depth = where.shape[0], parts[0].shape[1], operator.shape[1]
    in_specs = [pl.BlockSpec(p.shape, lambda i, w, a: (0, 0, 0), pipeline_mode=pl.Buffered(1)) for p in parts]
    in_specs.append(pl.BlockSpec((width, depth), lambda i, w, a: (w[i], 0)))
    return pl.pallas_call(
        functools.partial(product_kernel, len(parts), len(deps)),
        grid_spec=pltpu.PrefetchScalarGridSpec(
            num_scalar_prefetch=2,
            grid=(nb,),
            in_specs=in_specs + [HBM] * len(deps),
            out_specs=pl.BlockSpec((1, rows, width), lambda i, w, a: (i, 0, 0)),
            scratch_shapes=[pltpu.VMEM((2 * rows, depth), BF16)],
        ),
        out_shape=jax.ShapeDtypeStruct((nb, rows, width), F32),
        compiler_params=PARAMS,
        cost_estimate=cost(nb * rows * width * depth),
        name="product",
    )(where, at, *parts, operator, *deps)


def mix_kernel(groups, cut, coupling_ref, x_ref, *refs):
    outs = refs[-len(groups) * cut :]
    count, cases, width = x_ref.shape
    x_high, x_low = halves(x_ref[...].reshape(count * cases, width))
    shape = (count, count * cases)
    spread = lax.broadcasted_iota(jnp.int32, shape, 1) // cases == lax.broadcasted_iota(jnp.int32, shape, 0)
    shape = (cases, count * cases)
    own = lax.broadcasted_iota(jnp.int32, shape, 1) % cases == lax.broadcasted_iota(jnp.int32, shape, 0)
    wide = lax.dot_general(
        coupling_ref[...], spread.astype(F32), FIRST, precision=lax.Precision.HIGHEST, preferred_element_type=F32
    )
    part = width // cut
    for n, (first, held) in enumerate(groups):
        rows = [jnp.where(own, jnp.broadcast_to(wide[p : p + 1], shape), 0.0) for p in range(first, first + held)]
        high, low = halves(jnp.concatenate(rows, 0))
        mixed = dot(high, x_high, FIRST) + (dot(high, x_low, FIRST) + dot(low, x_high, FIRST))
        for h in range(cut):
            outs[n * cut + h][0] = mixed[:, h * part : (h + 1) * part]


def mix(coupling, modes, groups, cut, deps=()):
    count, cases, width = modes.shape
    shapes = [(1, held * cases, width // cut) for _, held in groups for _ in range(cut)]
    return pl.pallas_call(
        functools.partial(mix_kernel, groups, cut),
        grid=(1,),
        in_specs=[pl.BlockSpec(coupling.shape, lambda i: (0, 0)), pl.BlockSpec(modes.shape, lambda i: (0, 0, 0))]
        + [HBM] * len(deps),
        out_specs=[pl.BlockSpec(shape, lambda i: (0, 0, 0)) for shape in shapes],
        out_shape=[jax.ShapeDtypeStruct(shape, F32) for shape in shapes],
        compiler_params=PARAMS,
        cost_estimate=cost(0),
        name="mix",
    )(coupling, modes, *deps)


def place_kernel(first, x_ref, *refs):
    out_ref, done = refs[-2:]
    copy = pltpu.make_async_copy(x_ref, out_ref.at[pl.ds(first, x_ref.shape[0])], done)
    copy.start()
    copy.wait()


def place(x, shape, first, out):
    extra = [] if out is None else [out]
    return pl.pallas_call(
        functools.partial(place_kernel, first),
        grid=(1,),
        in_specs=[pl.BlockSpec(x.shape, lambda i: (0, 0, 0))] + [HBM] * len(extra),
        out_specs=HBM,
        out_shape=jax.ShapeDtypeStruct(shape, F32),
        scratch_shapes=[pltpu.SemaphoreType.DMA],
        input_output_aliases={1: 0} if extra else {},
        compiler_params=PARAMS,
        name="place",
    )(x, *extra)


def per_device(sizes, operator, modes, coupling):
    modes = jnp.transpose(modes, (1, 0, 2))
    count, cases, width = modes.shape
    n_row, n_col = lax.axis_size("row"), lax.axis_size("col")
    row, core = lax.axis_index("row"), lax.axis_index("col") % 2
    chips = jnp.arange(n_col // 2, dtype=jnp.int32)
    theirs, mine = chips * 2 + (1 - core), chips * 2 + core
    line = [list(range(c, n_col, 2)) for c in range(2)]
    cores = [(c, c ^ 1) for c in range(n_col)]
    starts = [sum(sizes[:g]) for g in range(len(sizes))]
    n, half, send = len(sizes), width // 2, lax.ppermute
    square = n_row == 4 and half % 128 == 0
    along_x = [(r, r ^ 1) for r in range(n_row)]
    along_y = [(r, r ^ 2) for r in range(n_row)]
    token, parts, sums, out = (), {}, {}, None
    at = jnp.stack([(row ^ f) * width + h * half for f in range(4) for h in range(2)]).astype(jnp.int32)

    def gather(groups, deps=()):
        nonlocal token
        mixed = mix(coupling, modes, [(starts[g], sizes[g]) for g in groups], 1, (*token, *deps))
        token = (mixed[0],)
        for g, chunk in zip(groups, mixed):
            parts[g] = [lax.all_gather(chunk, "row", axis=0 if square else 2, tiled=True)]

    def gather_first():
        nonlocal token
        left, right = mix(coupling, modes, [(0, sizes[0])], 2)
        token = (right,)
        xl, yr = send(left, "row", along_x), send(right, "row", along_y)
        xr, yl = send(right, "row", along_x), send(left, "row", along_y)
        dl, dr = send(xl, "row", along_y), send(yr, "row", along_x)
        parts[0] = [left, right, xl, xr, yl, yr, dl, dr]
        return xl, yr, xr, yl

    def run(g, where):
        nonlocal token
        x = product(parts[g], at, operator, width, where, token)
        token = (x,)
        return x

    if square:
        hops = gather_first()
        gather(range(1, 2), hops)
    else:
        gather(range(n))
    for g in range(n):
        ex = send(run(g, theirs), "col", cores)
        if g == 0 and square:
            gather(range(2, n))
        total = run(g, mine) + ex
        token = (total,)
        sums[g] = lax.psum_scatter(total, "col", scatter_dimension=0, axis_index_groups=line)
    for g in range(n):
        out = place(sums[g].reshape(sizes[g], cases, width), (count, cases, width), starts[g], out)
    return jnp.transpose(out, (1, 0, 2))


def solution(mesh):
    def on_each(operator, modes, coupling):
        return per_device(shares(coupling.shape[0]), operator, modes, coupling)

    in_specs = (P("row", "col"), P(None, None, ("col", "row")), P())
    out_specs = P(None, None, ("row", "col"))
    return jax.shard_map(on_each, mesh=mesh, in_specs=in_specs, out_specs=out_specs, check_vma=False)
```

time: 914 us -> 440 us (0.48)
  matrix products: 401 us -> 0 us
  waiting for transfers between devices: 496 us -> 130 us
  Pallas kernels: 0 us -> 256 us
  other arithmetic: 0 us -> 25.2 us
  starting transfers between devices: 0.04 us -> 9.72 us
    dot_general x2 -> x0, matrix products: 401 us -> none  [the longest x1 396 us: contract(): lax.dot_general(left, right, (((2,), (1,)), ((), ())), precision=lax.Prec...]
    pallas_call x0 -> x15, Pallas kernels: none -> 256 us  [the longest x8 226 us: product(): pl.pallas_call(functools.partial(product_kernel, len(parts), len(deps)),...]
    reduce_scatter x1 -> x4, waiting for transfers between devices: 336 us -> 112 us  [per_device(): lax.psum_scatter(total, 'col', scatter_dimension=0, axis_index_groups=line)]
    all_gather x1 -> x3, waiting for transfers between devices: 160 us -> 0.06 us  [gather(): lax.all_gather(chunk, 'row', axis=0 if square else 2, tiled=True)]
    add x0 -> x6, other arithmetic: none -> 25.2 us  [the longest x4 24.2 us: per_device(): total = run(g, mine) + ex]
    ppermute x0 -> x10, waiting for transfers between devices: none -> 16.5 us  [the longest x2 7.06 us: gather_first(): xr, yl = (send(right, 'row', along_x), send(left, 'row', along_y))]
  transfers between devices with their start and end apart: 2 -> 17, of which waited for: 2 -> 7; matrix products, arithmetic and copies ran while one was open for 0% -> 6% of each run, Pallas kernels for 0% -> 56%
where the time goes in v1:
time: 440 us; the launch traced here: 436 us
  Pallas kernels  256 us (58%)
  waiting for transfers between devices  130 us (30%)
  other arithmetic  25.2 us (6%)
  between operations  15.1 us (3%)
  starting transfers between devices  9.72 us (2%)
    pallas_call x8, Pallas kernels, product(): pl.pallas_call(functools.partial(product_kernel, len(parts), len(deps)),...  226 us
    reduce_scatter x4, waiting for transfers between devices, per_device(): lax.psum_scatter(total, 'col', scatter_dimension=0, axis_index_groups=line)  112 us
    add x4, other arithmetic, per_device(): total = run(g, mine) + ex  24.2 us
    pallas_call x3, Pallas kernels, mix(): pl.pallas_call(functools.partial(mix_kernel, groups, cut), grid=(1,), in_...  21 us
  transfers between devices with their start and end apart: 17, of which 7 were waited for; matrix products, arithmetic and copies ran while one was open for 6% of the time, Pallas kernels for 56%

profile of v1, /device:TPU:0, one launch (start us, length us, event | category | flops | bytes accessed | tf_op | source)
XLA Modules:
  0.0 436.0 jit_solution(11907487297339052948)
XLA Ops:
  7.4 4.9 %mix.3 = (f32[1,176,384]{2,1,0:T(8,128)}, f32[1,176,384]{2,1,0:T(8,128)}) custom-call(f32[84,84]{1,0:T(8,128)} %coupling_ref.5, f32[84,16,768]{2,1,0:T(8,128)} %bitcast.14), custom_call_target="tpu_custom_call" | custom-call | tf_op jit(solution)/shard_map/mix/pallas_call | solution.py:99
  12.2 3.0 collective-permute-start.2
  17.2 5.6 %collective-permute-done.2.refs_4_ = f32[1,176,384]{2,1,0:T(8,128)} collective-permute-done((f32[1,176,384]{2,1,0:T(8,128)}, f32[1,176,384]{2,1,0:T(8,128)}, u32[]{:S(2)}, u32[]{:S(2)}) %collective-permute-start.2) | collective-permute-done | bytes 270368 | tf_op jit(solution)/shard_map/ppermute | solution.py:163
  22.8 2.1 collective-permute-done.refs_1_.refs_2_
  24.9 2.9 collective-permute-done.3.refs_2_.refs_5_
  29.3 5.5 %mix.4.refs_9_ = f32[1,240,768]{2,1,0:T(8,128)} custom-call(f32[84,84]{1,0:T(8,128)} %coupling_ref.5, f32[84,16,768]{2,1,0:T(8,128)} %bitcast.15, f32[1,176,384]{2,1,0:T(8,128)} %get-tuple-element.10.refs_0_.refs_1_, f32[1,176,384]{2,1,0:T(8,128)} %collective-permute-done.refs_1_.refs_2_, f32[1,176,384]{2,1,0:T(8,128)} %collective-permute-done.3.refs_2_.refs_5_, ...), custom_call_target="tpu_custom_call" | custom-call | tf_op jit(solution)/shard_map/mix/pallas_call | solution.py:99
  38.6 4.2 collective-permute-done.4.refs_6_
  43.1 20.2 %product.8.refs_0_ = f32[4,176,768]{2,1,0:T(8,128)} custom-call(s32[4]{0:T(128)} %fusion.where_ref, s32[8]{0:T(128)} %stack.35.at_ref, f32[1,176,384]{2,1,0:T(8,128)} %get-tuple-element.9.refs_0_, f32[1,176,384]{2,1,0:T(8,128)} %get-tuple-element.10.refs_0_.refs_1_, f32[1,176,384]{2,1,0:T(8,128)} %collective-permute-done.refs_1_.refs_2_, ...), custom_call_target="tpu_custom_call" | custom-call | flops 9965666304 | tf_op jit(solution)/shard_map/product/pallas_call | solution.py:60
  63.3 10.6 %mix.5 = (f32[1,400,768]{2,1,0:T(8,128)}, f32[1,528,768]{2,1,0:T(8,128)}) custom-call(f32[84,84]{1,0:T(8,128)} %coupling_ref.5, f32[84,16,768]{2,1,0:T(8,128)} %bitcast.16, f32[4,176,768]{2,1,0:T(8,128)} %product.8.refs_0_), custom_call_target="tpu_custom_call" | custom-call | tf_op jit(solution)/shard_map/mix/pallas_call | solution.py:99
  75.5 21.1 %product.9 = f32[4,176,768]{2,1,0:T(8,128)} custom-call(s32[4]{0:T(128)} %fusion.1.where_ref, s32[8]{0:T(128)} %stack.35.at_ref, f32[1,176,384]{2,1,0:T(8,128)} %get-tuple-element.9.refs_0_, f32[1,176,384]{2,1,0:T(8,128)} %get-tuple-element.10.refs_0_.refs_1_, f32[1,176,384]{2,1,0:T(8,128)} %collective-permute-done.refs_1_.refs_2_, ...), custom_call_target="tpu_custom_call" | custom-call | flops 9965666304 | tf_op jit(solution)/shard_map/product/pallas_call | solution.py:60
  96.6 3.9 add.57.refs_2_
  100.6 21.7 %product.10.refs_2_ = f32[4,240,768]{2,1,0:T(8,128)} custom-call(s32[4]{0:T(128)} %fusion.where_ref, s32[8]{0:T(128)} %stack.35.at_ref, f32[4,240,768]{2,1,0:T(8,128)} %all-gather.8.cloned.1.call-done.refs_0_, f32[6144,3072]{1,0:T(8,128)} %refs_1_.11, f32[4,176,768]{2,1,0:T(8,128)} %add.57.refs_2_), custom_call_target="tpu_custom_call" | custom-call | flops 13589544960 | tf_op jit(solution)/shard_map/product/pallas_call | solution.py:60
  122.9 21.8 %product.11 = f32[4,240,768]{2,1,0:T(8,128)} custom-call(s32[4]{0:T(128)} %fusion.1.where_ref, s32[8]{0:T(128)} %stack.35.at_ref, f32[4,240,768]{2,1,0:T(8,128)} %all-gather.8.cloned.1.call-done.refs_0_, f32[6144,3072]{1,0:T(8,128)} %refs_1_.11, f32[4,240,768]{2,1,0:T(8,128)} %product.10.refs_2_), custom_call_target="tpu_custom_call" | custom-call | flops 13589544960 | tf_op jit(solution)/shard_map/product/pallas_call | solution.py:60
  144.7 5.1 %add.58.refs_2_ = f32[4,240,768]{2,1,0:T(8,128)} add(f32[4,240,768]{2,1,0:T(8,128)} %product.11, f32[4,240,768]{2,1,0:T(8,128)} %collective-permute-done.7) | non-fusion elementwise | flops 737280 | bytes 8847360 | tf_op jit(solution)/shard_map/add | solution.py:183
  150.1 31.1 %product.12.refs_2_ = f32[4,400,768]{2,1,0:T(8,128)} custom-call(s32[4]{0:T(128)} %fusion.where_ref, s32[8]{0:T(128)} %stack.35.at_ref, f32[4,400,768]{2,1,0:T(8,128)} %all-gather.6.cloned.1.call-done.refs_0_, f32[6144,3072]{1,0:T(8,128)} %refs_1_.11, f32[4,240,768]{2,1,0:T(8,128)} %add.58.refs_2_), custom_call_target="tpu_custom_call" | custom-call | flops 22649241600 | tf_op jit(solution)/shard_map/product/pallas_call | solution.py:60
  181.3 31.2 %product.13 = f32[4,400,768]{2,1,0:T(8,128)} custom-call(s32[4]{0:T(128)} %fusion.1.where_ref, s32[8]{0:T(128)} %stack.35.at_ref, f32[4,400,768]{2,1,0:T(8,128)} %all-gather.6.cloned.1.call-done.refs_0_, f32[6144,3072]{1,0:T(8,128)} %refs_1_.11, f32[4,400,768]{2,1,0:T(8,128)} %product.12.refs_2_), custom_call_target="tpu_custom_call" | custom-call | flops 22649241600 | tf_op jit(solution)/shard_map/product/pallas_call | solution.py:60
  212.5 6.8 %add.59.refs_2_ = f32[4,400,768]{2,1,0:T(8,128)} add(f32[4,400,768]{2,1,0:T(8,128)} %product.13, f32[4,400,768]{2,1,0:T(8,128)} %collective-permute-done.8) | non-fusion elementwise | flops 1228800 | bytes 14745600 | tf_op jit(solution)/shard_map/add | solution.py:183
  219.8 39.2 %product.14.refs_2_ = f32[4,528,768]{2,1,0:T(8,128)} custom-call(s32[4]{0:T(128)} %fusion.where_ref, s32[8]{0:T(128)} %stack.35.at_ref, f32[4,528,768]{2,1,0:T(8,128)} %all-gather.4.cloned.1.call-done.refs_0_, f32[6144,3072]{1,0:T(8,128)} %refs_1_.11, f32[4,400,768]{2,1,0:T(8,128)} %add.59.refs_2_), custom_call_target="tpu_custom_call" | custom-call | flops 29896998912 | tf_op jit(solution)/shard_map/product/pallas_call | solution.py:60
  259.5 39.5 %product.15 = f32[4,528,768]{2,1,0:T(8,128)} custom-call(s32[4]{0:T(128)} %fusion.1.where_ref, s32[8]{0:T(128)} %stack.35.at_ref, f32[4,528,768]{2,1,0:T(8,128)} %all-gather.4.cloned.1.call-done.refs_0_, f32[6144,3072]{1,0:T(8,128)} %refs_1_.11, f32[4,528,768]{2,1,0:T(8,128)} %product.14.refs_2_), custom_call_target="tpu_custom_call" | custom-call | flops 29896998912 | tf_op jit(solution)/shard_map/product/pallas_call | solution.py:60
  299.0 8.4 %add.60 = f32[4,528,768]{2,1,0:T(8,128)} add(f32[4,528,768]{2,1,0:T(8,128)} %product.15, f32[4,528,768]{2,1,0:T(8,128)} %collective-permute-done.9) | non-fusion elementwise | flops 1622016 | bytes 19464192 | tf_op jit(solution)/shard_map/add | solution.py:183
  309.4 2.0 place.5.refs_0_
  311.4 2.3 place.6.refs_0_
  313.7 112.1 %reduce-scatter.5.cloned.1.call-done = f32[1,528,768]{2,1,0:T(8,128)} async-done(((f32[4,528,768]{2,1,0:T(8,128)}), f32[1,528,768]{2,1,0:T(8,128)}) %reduce-scatter.5.cloned.1.call-update) | async-done | bytes 1622032 | tf_op jit(solution)/shard_map/reduce_scatter | solution.py:185
  425.8 2.6 place.7
  (39 shorter events, 13.0 us)
Async XLA Ops:
  7.4 93.2 %all-gather.8.cloned.1.call-start = ((), (), s32[]{:S(2)}) async-start(), calls=%async_computation.6 | async-start | bytes 3686400 | tf_op jit(solution)/shard_map/all_gather | solution.py:156
  12.2 10.6 %collective-permute-start.2 = (f32[1,176,384]{2,1,0:T(8,128)}, f32[1,176,384]{2,1,0:T(8,128)}, u32[]{:S(2)}, u32[]{:S(2)}) collective-permute-start(f32[1,176,384]{2,1,0:T(8,128)} %get-tuple-element.9.refs_0_), channel_id=1, source_target_pairs={{0,16},{8,24},{16,0},{24,8},{1,17},{9,25},{17,1},{25,9},{2,18},{10... | collective-permute-start | bytes 811016 | tf_op jit(solution)/shard_map/ppermute | solution.py:163
  15.2 9.7 %collective-permute-start = (f32[1,176,384]{2,1,0:T(8,128)}, f32[1,176,384]{2,1,0:T(8,128)}, u32[]{:S(2)}, u32[]{:S(2)}) collective-permute-start(f32[1,176,384]{2,1,0:T(8,128)} %get-tuple-element.9.refs_0_), channel_id=1, source_target_pairs={{0,8},{8,0},{16,24},{24,16},{1,9},{9,1},{17,25},{25,17},{2,10},{10... | collective-permute-start | bytes 811016 | tf_op jit(solution)/shard_map/ppermute | solution.py:162
  16.7 11.1 %collective-permute-start.3 = (f32[1,176,384]{2,1,0:T(8,128)}, f32[1,176,384]{2,1,0:T(8,128)}, u32[]{:S(2)}, u32[]{:S(2)}) collective-permute-start(f32[1,176,384]{2,1,0:T(8,128)} %get-tuple-element.10.refs_0_.refs_1_), channel_id=1, source_target_pairs={{0,16},{8,24},{16,0},{24,8},{1,17},{9,25},{17,1},{25,9},{2,18},{10... | collective-permute-start | bytes 811016 | tf_op jit(solution)/shard_map/ppermute | solution.py:162
  17.2 12.0 %collective-permute-start.1 = (f32[1,176,384]{2,1,0:T(8,128)}, f32[1,176,384]{2,1,0:T(8,128)}, u32[]{:S(2)}, u32[]{:S(2)}) collective-permute-start(f32[1,176,384]{2,1,0:T(8,128)} %get-tuple-element.10.refs_0_.refs_1_), channel_id=1, source_target_pairs={{0,8},{8,0},{16,24},{24,16},{1,9},{9,1},{17,25},{25,17},{2,10},{10... | collective-permute-start | bytes 811016 | tf_op jit(solution)/shard_map/ppermute | solution.py:163
  34.8 115.4 %all-gather.6.cloned.1.call-start = ((), (), s32[]{:S(2)}) async-start(), calls=%async_computation.5 | async-start | bytes 6144000 | tf_op jit(solution)/shard_map/all_gather | solution.py:156
  35.3 7.4 %collective-permute-start.4 = (f32[1,176,384]{2,1,0:T(8,128)}, f32[1,176,384]{2,1,0:T(8,128)}, u32[]{:S(2)}, u32[]{:S(2)}) collective-permute-start(f32[1,176,384]{2,1,0:T(8,128)} %collective-permute-done.refs_1_.refs_2_), channel_id=1, source_target_pairs={{0,16},{8,24},{16,0},{24,8},{1,17},{9,25},{17,1},{25,9},{2,18},{10... | collective-permute-start | bytes 811016 | tf_op jit(solution)/shard_map/ppermute | solution.py:164
  35.7 7.4 %collective-permute-start.5 = (f32[1,176,384]{2,1,0:T(8,128)}, f32[1,176,384]{2,1,0:T(8,128)}, u32[]{:S(2)}, u32[]{:S(2)}) collective-permute-start(f32[1,176,384]{2,1,0:T(8,128)} %collective-permute-done.3.refs_2_.refs_5_), channel_id=1, source_target_pairs={{0,8},{8,0},{16,24},{24,16},{1,9},{9,1},{17,25},{25,17},{2,10},{10... | collective-permute-start | bytes 811016 | tf_op jit(solution)/shard_map/ppermute | solution.py:164
  73.9 145.9 %all-gather.4.cloned.1.call-start = ((), (), s32[]{:S(2)}) async-start(), calls=%async_computation.4 | async-start | bytes 8110080 | tf_op jit(solution)/shard_map/all_gather | solution.py:156
  74.6 232.8 %reduce-scatter.11.cloned.1.call-start = ((), (), s32[]{:S(2)}) async-start(), calls=%async_computation.10 | async-start | bytes 2703360 | tf_op jit(solution)/shard_map/reduce_scatter | solution.py:185
  74.9 21.8 %collective-permute-start.6 = (f32[4,176,768]{2,1,0:T(8,128)}, f32[4,176,768]{2,1,0:T(8,128)}, u32[]{:S(2)}, u32[]{:S(2)}) collective-permute-start(f32[4,176,768]{2,1,0:T(8,128)} %product.8.refs_0_), channel_id=1, source_target_pairs={{0,1},{1,0},{2,3},{3,2},{4,5},{5,4},{6,7},{7,6},{8,9},{9,8},{10,11... | collective-permute-start | bytes 6488072 | tf_op jit(solution)/shard_map/ppermute | solution.py:180
  100.5 208.8 %reduce-scatter.9.cloned.1.call-start = ((), (), s32[]{:S(2)}) async-start(), calls=%async_computation.9 | async-start | bytes 3686400 | tf_op jit(solution)/shard_map/reduce_scatter | solution.py:185
  122.3 22.3 %collective-permute-start.7 = (f32[4,240,768]{2,1,0:T(8,128)}, f32[4,240,768]{2,1,0:T(8,128)}, u32[]{:S(2)}, u32[]{:S(2)}) collective-permute-start(f32[4,240,768]{2,1,0:T(8,128)} %product.10.refs_2_), channel_id=1, source_target_pairs={{0,1},{1,0},{2,3},{3,2},{4,5},{5,4},{6,7},{7,6},{8,9},{9,8},{10,11... | collective-permute-start | bytes 8847368 | tf_op jit(solution)/shard_map/ppermute | solution.py:180
  149.9 161.5 %reduce-scatter.7.cloned.1.call-start = ((), (), s32[]{:S(2)}) async-start(), calls=%async_computation.8 | async-start | bytes 6144000 | tf_op jit(solution)/shard_map/reduce_scatter | solution.py:185
  181.3 31.2 %collective-permute-start.8 = (f32[4,400,768]{2,1,0:T(8,128)}, f32[4,400,768]{2,1,0:T(8,128)}, u32[]{:S(2)}, u32[]{:S(2)}) collective-permute-start(f32[4,400,768]{2,1,0:T(8,128)} %product.12.refs_2_), channel_id=1, source_target_pairs={{0,1},{1,0},{2,3},{3,2},{4,5},{5,4},{6,7},{7,6},{8,9},{9,8},{10,11... | collective-permute-start | bytes 14745608 | tf_op jit(solution)/shard_map/ppermute | solution.py:180
  219.3 206.5 %reduce-scatter.5.cloned.1.call-start = ((), (), s32[]{:S(2)}) async-start(), calls=%async_computation.7 | async-start | bytes 8110080 | tf_op jit(solution)/shard_map/reduce_scatter | solution.py:185
  259.0 40.0 %collective-permute-start.9 = (f32[4,528,768]{2,1,0:T(8,128)}, f32[4,528,768]{2,1,0:T(8,128)}, u32[]{:S(2)}, u32[]{:S(2)}) collective-permute-start(f32[4,528,768]{2,1,0:T(8,128)} %product.14.refs_2_), channel_id=1, source_target_pairs={{0,1},{1,0},{2,3},{3,2},{4,5},{5,4},{6,7},{7,6},{8,9},{9,8},{10,11... | collective-permute-start | bytes 19464200 | tf_op jit(solution)/shard_map/ppermute | solution.py:180
Sparse Core Ops, SparseCore 0:
  34.9 42.6 all-gather.7
  79.4 58.6 all-gather.5
  140.2 71.7 all-gather.3
Sparse Core Ops, SparseCore 1:
  100.6 45.8 reduce-scatter.10
  149.9 58.3 reduce-scatter.8
  219.4 89.6 reduce-scatter.6
  311.5 114.3 reduce-scatter.4

commit v2 on v1

--- a/solution.py
+++ b/solution.py
@@ -7,7 +7,7 @@
 from jax.experimental.pallas import tpu as pltpu
 from jax.sharding import PartitionSpec as P
 
-CUTS = (0.131, 0.31, 0.607)
+CUTS = (0.155, 0.36, 0.63)
 F32, BF16 = jnp.float32, jnp.bfloat16
 LAST = (((1,), (1,)), ((), ()))
 FIRST = (((1,), (0,)), ((), ()))
@@ -104,9 +104,27 @@
         out_specs=[pl.BlockSpec(shape, lambda i: (0, 0, 0)) for shape in shapes],
         out_shape=[jax.ShapeDtypeStruct(shape, F32) for shape in shapes],
         compiler_params=PARAMS,
-        cost_estimate=cost(0),
+        cost_estimate=cost(sum(held for _, held in groups) * cases * count * cases * width),
         name="mix",
     )(coupling, modes, *deps)
+
+
+def gate_kernel(*refs):
+    del refs
+
+
+def gate(arrays, deps):
+    n = len(arrays)
+    return pl.pallas_call(
+        gate_kernel,
+        in_specs=[HBM] * (n + len(deps)),
+        out_specs=[HBM] * n,
+        out_shape=[jax.ShapeDtypeStruct(x.shape, x.dtype) for x in arrays],
+        input_output_aliases={i: i for i in range(n)},
+        compiler_params=PARAMS,
+        cost_estimate=cost(0),
+        name="gate",
+    )(*arrays, *deps)
 
 
 def place_kernel(first, x_ref, *refs):
@@ -148,11 +166,15 @@
     token, parts, sums, out = (), {}, {}, None
     at = jnp.stack([(row ^ f) * width + h * half for f in range(4) for h in range(2)]).astype(jnp.int32)
 
-    def gather(groups, deps=()):
+    def mixed(groups):
+        chunks = mix(coupling, modes, [(starts[g], sizes[g]) for g in groups], 1, token)
+        return dict(zip(groups, chunks))
+
+    def gather(chunks, deps):
         nonlocal token
-        mixed = mix(coupling, modes, [(starts[g], sizes[g]) for g in groups], 1, (*token, *deps))
-        token = (mixed[0],)
-        for g, chunk in zip(groups, mixed):
+        gated = gate(list(chunks.values()), (*token, *deps))
+        token = (gated[0],)
+        for g, chunk in zip(chunks, gated):
             parts[g] = [lax.all_gather(chunk, "row", axis=0 if square else 2, tiled=True)]
 
     def gather_first():
@@ -173,13 +195,14 @@
 
     if square:
         hops = gather_first()
-        gather(range(1, 2), hops)
+        chunks = mixed(range(1, n))
+        gather({g: chunks[g] for g in (1,)}, hops)
     else:
-        gather(range(n))
+        gather(mixed(range(n)), ())
     for g in range(n):
         ex = send(run(g, theirs), "col", cores)
         if g == 0 and square:
-            gather(range(2, n))
+            gather({g: chunks[g] for g in range(2, n)}, ())
         total = run(g, mine) + ex
         token = (total,)
         sums[g] = lax.psum_scatter(total, "col", scatter_dimension=0, axis_index_groups=line)

time: 440 us -> 418 us (0.950)
  waiting for transfers between devices: 130 us -> 113 us
  Pallas kernels: 256 us -> 248 us
    reduce_scatter x4, waiting for transfers between devices: 112 us -> 104 us  [per_device(): lax.psum_scatter(total, 'col', scatter_dimension=0, axis_index_groups=line)]
    ppermute x2, waiting for transfers between devices: 7.06 us -> 1.47 us  [gather_first(): xr, yl = (send(right, 'row', along_x), send(left, 'row', along_y))]
    pallas_call x3 -> x2, Pallas kernels: 21 us -> 17.2 us  [mix(): pl.pallas_call(functools.partial(mix_kernel, groups, cut), grid=(1,), in_...]
  transfers between devices with their start and end apart: 17 -> 17, of which waited for: 7 -> 5; matrix products, arithmetic and copies ran while one was open for 6% -> 6% of each run, Pallas kernels for 56% -> 58%
where the time goes in v2:
time: 418 us; the launch traced here: 410 us
  Pallas kernels  248 us (59%)
  waiting for transfers between devices  113 us (27%)
  other arithmetic  24.7 us (6%)
  between operations  15.2 us (4%)
  starting transfers between devices  9.53 us (2%)
    pallas_call x8, Pallas kernels, product(): pl.pallas_call(functools.partial(product_kernel, len(parts), len(deps)),...  222 us
    reduce_scatter x4, waiting for transfers between devices, per_device(): lax.psum_scatter(total, 'col', scatter_dimension=0, axis_index_groups=line)  104 us
    add x4, other arithmetic, per_device(): total = run(g, mine) + ex  23.7 us
    pallas_call x2, Pallas kernels, mix(): pl.pallas_call(functools.partial(mix_kernel, groups, cut), grid=(1,), in_...  17.2 us
    pallas_call x4, Pallas kernels, place(): pl.pallas_call(functools.partial(place_kernel, first), grid=(1,), in_spec...  8.76 us
  transfers between devices with their start and end apart: 17, of which 5 were waited for; matrix products, arithmetic and copies ran while one was open for 6% of the time, Pallas kernels for 58%

profile of v2, /device:TPU:0, one launch (start us, length us, event | category | flops | bytes accessed | tf_op | source)
XLA Modules:
  0.0 410.3 jit_solution(11390104376740482030)
XLA Ops:
  7.4 5.1 %mix.2 = (f32[1,208,384]{2,1,0:T(8,128)}, f32[1,208,384]{2,1,0:T(8,128)}) custom-call(f32[84,84]{1,0:T(8,128)} %coupling_ref.3, f32[84,16,768]{2,1,0:T(8,128)} %bitcast.18), custom_call_target="tpu_custom_call" | custom-call | flops 1288175616 | tf_op jit(solution)/shard_map/mix/pallas_call | solution.py:99
  12.5 3.0 collective-permute-start.2
  15.5 1.5 collective-permute-start
  17.5 12.0 %mix.3 = (f32[1,272,768]{2,1,0:T(8,128)}, f32[1,368,768]{2,1,0:T(8,128)}, f32[1,496,768]{2,1,0:T(8,128)}) custom-call(f32[84,84]{1,0:T(8,128)} %coupling_ref.3, f32[84,16,768]{2,1,0:T(8,128)} %bitcast.19, f32[1,208,384]{2,1,0:T(8,128)} %get-tuple-element.12.refs_0_.refs_1_), custom_call_target="tpu_custom_call" | custom-call | flops 7035420672 | tf_op jit(solution)/shard_map/mix/pallas_call | solution.py:99
  30.2 1.5 collective-permute-done.1.refs_4_.refs_3_
  32.3 1.7 collective-permute-start.5
  35.2 5.2 %collective-permute-done.4.refs_6_ = f32[1,208,384]{2,1,0:T(8,128)} collective-permute-done((f32[1,208,384]{2,1,0:T(8,128)}, f32[1,208,384]{2,1,0:T(8,128)}, u32[]{:S(2)}, u32[]{:S(2)}) %collective-permute-start.4) | collective-permute-done | bytes 319520 | tf_op jit(solution)/shard_map/ppermute | solution.py:186
  40.8 20.6 %product.8.refs_2_ = f32[4,208,768]{2,1,0:T(8,128)} custom-call(s32[4]{0:T(128)} %fusion.where_ref, s32[8]{0:T(128)} %stack.35.at_ref, f32[1,208,384]{2,1,0:T(8,128)} %get-tuple-element.15.refs_0_, f32[1,208,384]{2,1,0:T(8,128)} %get-tuple-element.12.refs_0_.refs_1_, f32[1,208,384]{2,1,0:T(8,128)} %collective-permute-done.refs_2_, ...), custom_call_target="tpu_custom_call" | custom-call | flops 11777605632 | tf_op jit(solution)/shard_map/product/pallas_call | solution.py:60
  62.8 20.6 %product.9 = f32[4,208,768]{2,1,0:T(8,128)} custom-call(s32[4]{0:T(128)} %fusion.1.where_ref, s32[8]{0:T(128)} %stack.35.at_ref, f32[1,208,384]{2,1,0:T(8,128)} %get-tuple-element.15.refs_0_, f32[1,208,384]{2,1,0:T(8,128)} %get-tuple-element.12.refs_0_.refs_1_, f32[1,208,384]{2,1,0:T(8,128)} %collective-permute-done.refs_2_, ...), custom_call_target="tpu_custom_call" | custom-call | flops 11777605632 | tf_op jit(solution)/shard_map/product/pallas_call | solution.py:60
  83.4 4.2 %add.57.refs_2_ = f32[4,208,768]{2,1,0:T(8,128)} add(f32[4,208,768]{2,1,0:T(8,128)} %product.9, f32[4,208,768]{2,1,0:T(8,128)} %collective-permute-done.6) | non-fusion elementwise | flops 638976 | bytes 7667712 | tf_op jit(solution)/shard_map/add | solution.py:206
  88.3 23.1 %product.10.refs_2_ = f32[4,272,768]{2,1,0:T(8,128)} custom-call(s32[4]{0:T(128)} %fusion.where_ref, s32[8]{0:T(128)} %stack.35.at_ref, f32[4,272,768]{2,1,0:T(8,128)} %all-gather.8.cloned.1.call-done.refs_0_, f32[6144,3072]{1,0:T(8,128)} %refs_1_.11, f32[4,208,768]{2,1,0:T(8,128)} %add.57.refs_2_), custom_call_target="tpu_custom_call" | custom-call | flops 15401484288 | tf_op jit(solution)/shard_map/product/pallas_call | solution.py:60
  111.9 23.1 %product.11 = f32[4,272,768]{2,1,0:T(8,128)} custom-call(s32[4]{0:T(128)} %fusion.1.where_ref, s32[8]{0:T(128)} %stack.35.at_ref, f32[4,272,768]{2,1,0:T(8,128)} %all-gather.8.cloned.1.call-done.refs_0_, f32[6144,3072]{1,0:T(8,128)} %refs_1_.11, f32[4,272,768]{2,1,0:T(8,128)} %product.10.refs_2_), custom_call_target="tpu_custom_call" | custom-call | flops 15401484288 | tf_op jit(solution)/shard_map/product/pallas_call | solution.py:60
  135.1 5.2 %add.58.refs_2_ = f32[4,272,768]{2,1,0:T(8,128)} add(f32[4,272,768]{2,1,0:T(8,128)} %product.11, f32[4,272,768]{2,1,0:T(8,128)} %collective-permute-done.7) | non-fusion elementwise | flops 835584 | bytes 10027008 | tf_op jit(solution)/shard_map/add | solution.py:206
  140.5 30.3 %product.12.refs_2_ = f32[4,368,768]{2,1,0:T(8,128)} custom-call(s32[4]{0:T(128)} %fusion.where_ref, s32[8]{0:T(128)} %stack.35.at_ref, f32[4,368,768]{2,1,0:T(8,128)} %all-gather.6.cloned.1.call-done.refs_0_, f32[6144,3072]{1,0:T(8,128)} %refs_1_.11, f32[4,272,768]{2,1,0:T(8,128)} %add.58.refs_2_), custom_call_target="tpu_custom_call" | custom-call | flops 20837302272 | tf_op jit(solution)/shard_map/product/pallas_call | solution.py:60
  170.8 29.3 %product.13 = f32[4,368,768]{2,1,0:T(8,128)} custom-call(s32[4]{0:T(128)} %fusion.1.where_ref, s32[8]{0:T(128)} %stack.35.at_ref, f32[4,368,768]{2,1,0:T(8,128)} %all-gather.6.cloned.1.call-done.refs_0_, f32[6144,3072]{1,0:T(8,128)} %refs_1_.11, f32[4,368,768]{2,1,0:T(8,128)} %product.12.refs_2_), custom_call_target="tpu_custom_call" | custom-call | flops 20837302272 | tf_op jit(solution)/shard_map/product/pallas_call | solution.py:60
  200.1 6.4 %add.59.refs_2_ = f32[4,368,768]{2,1,0:T(8,128)} add(f32[4,368,768]{2,1,0:T(8,128)} %product.13, f32[4,368,768]{2,1,0:T(8,128)} %collective-permute-done.8) | non-fusion elementwise | flops 1130496 | bytes 13565952 | tf_op jit(solution)/shard_map/add | solution.py:206
  206.8 37.2 %product.14.refs_2_ = f32[4,496,768]{2,1,0:T(8,128)} custom-call(s32[4]{0:T(128)} %fusion.where_ref, s32[8]{0:T(128)} %stack.35.at_ref, f32[4,496,768]{2,1,0:T(8,128)} %all-gather.4.cloned.1.call-done.refs_0_, f32[6144,3072]{1,0:T(8,128)} %refs_1_.11, f32[4,368,768]{2,1,0:T(8,128)} %add.59.refs_2_), custom_call_target="tpu_custom_call" | custom-call | flops 28085059584 | tf_op jit(solution)/shard_map/product/pallas_call | solution.py:60
  244.4 37.4 %product.15 = f32[4,496,768]{2,1,0:T(8,128)} custom-call(s32[4]{0:T(128)} %fusion.1.where_ref, s32[8]{0:T(128)} %stack.35.at_ref, f32[4,496,768]{2,1,0:T(8,128)} %all-gather.4.cloned.1.call-done.refs_0_, f32[6144,3072]{1,0:T(8,128)} %refs_1_.11, f32[4,496,768]{2,1,0:T(8,128)} %product.14.refs_2_), custom_call_target="tpu_custom_call" | custom-call | flops 28085059584 | tf_op jit(solution)/shard_map/product/pallas_call | solution.py:60
  281.8 7.9 %add.60 = f32[4,496,768]{2,1,0:T(8,128)} add(f32[4,496,768]{2,1,0:T(8,128)} %product.15, f32[4,496,768]{2,1,0:T(8,128)} %collective-permute-done.9) | non-fusion elementwise | flops 1523712 | bytes 18284544 | tf_op jit(solution)/shard_map/add | solution.py:206
  289.8 1.9 place.4.refs_0_
  291.7 2.1 place.5.refs_0_
  293.8 2.3 place.6.refs_0_
  296.1 104.1 %reduce-scatter.5.cloned.1.call-done = f32[1,496,768]{2,1,0:T(8,128)} async-done(((f32[4,496,768]{2,1,0:T(8,128)}), f32[1,496,768]{2,1,0:T(8,128)}) %reduce-scatter.5.cloned.1.call-update) | async-done | bytes 1523728 | tf_op jit(solution)/shard_map/reduce_scatter | solution.py:208
  400.2 2.5 place.7
  (40 shorter events, 6.9 us)
Async XLA Ops:
  7.4 80.9 %all-gather.8.cloned.1.call-start = ((), (), s32[]{:S(2)}) async-start(), calls=%async_computation.6 | async-start | bytes 4177920 | tf_op jit(solution)/shard_map/all_gather | solution.py:178
  12.5 17.0 %collective-permute-start.2 = (f32[1,208,384]{2,1,0:T(8,128)}, f32[1,208,384]{2,1,0:T(8,128)}, u32[]{:S(2)}, u32[]{:S(2)}) collective-permute-start(f32[1,208,384]{2,1,0:T(8,128)} %get-tuple-element.15.refs_0_), channel_id=1, source_target_pairs={{0,16},{8,24},{16,0},{24,8},{1,17},{9,25},{17,1},{25,9},{2,18},{10... | collective-permute-start | bytes 958472 | tf_op jit(solution)/shard_map/ppermute | solution.py:185
  15.5 14.1 %collective-permute-start = (f32[1,208,384]{2,1,0:T(8,128)}, f32[1,208,384]{2,1,0:T(8,128)}, u32[]{:S(2)}, u32[]{:S(2)}) collective-permute-start(f32[1,208,384]{2,1,0:T(8,128)} %get-tuple-element.15.refs_0_), channel_id=1, source_target_pairs={{0,8},{8,0},{16,24},{24,16},{1,9},{9,1},{17,25},{25,17},{2,10},{10... | collective-permute-start | bytes 958472 | tf_op jit(solution)/shard_map/ppermute | solution.py:184
  17.0 13.2 %collective-permute-start.3 = (f32[1,208,384]{2,1,0:T(8,128)}, f32[1,208,384]{2,1,0:T(8,128)}, u32[]{:S(2)}, u32[]{:S(2)}) collective-permute-start(f32[1,208,384]{2,1,0:T(8,128)} %get-tuple-element.12.refs_0_.refs_1_), channel_id=1, source_target_pairs={{0,16},{8,24},{16,0},{24,8},{1,17},{9,25},{17,1},{25,9},{2,18},{10... | collective-permute-start | bytes 958472 | tf_op jit(solution)/shard_map/ppermute | solution.py:184
  17.5 14.2 %collective-permute-start.1 = (f32[1,208,384]{2,1,0:T(8,128)}, f32[1,208,384]{2,1,0:T(8,128)}, u32[]{:S(2)}, u32[]{:S(2)}) collective-permute-start(f32[1,208,384]{2,1,0:T(8,128)} %get-tuple-element.12.refs_0_.refs_1_), channel_id=1, source_target_pairs={{0,8},{8,0},{16,24},{24,16},{1,9},{9,1},{17,25},{25,17},{2,10},{10... | collective-permute-start | bytes 958472 | tf_op jit(solution)/shard_map/ppermute | solution.py:185
  31.7 108.8 %all-gather.6.cloned.1.call-start = ((), (), s32[]{:S(2)}) async-start(), calls=%async_computation.5 | async-start | bytes 5652480 | tf_op jit(solution)/shard_map/all_gather | solution.py:178
  32.0 8.5 %collective-permute-start.4 = (f32[1,208,384]{2,1,0:T(8,128)}, f32[1,208,384]{2,1,0:T(8,128)}, u32[]{:S(2)}, u32[]{:S(2)}) collective-permute-start(f32[1,208,384]{2,1,0:T(8,128)} %collective-permute-done.refs_2_), channel_id=1, source_target_pairs={{0,16},{8,24},{16,0},{24,8},{1,17},{9,25},{17,1},{25,9},{2,18},{10... | collective-permute-start | bytes 958472 | tf_op jit(solution)/shard_map/ppermute | solution.py:186
  32.3 8.4 %collective-permute-start.5 = (f32[1,208,384]{2,1,0:T(8,128)}, f32[1,208,384]{2,1,0:T(8,128)}, u32[]{:S(2)}, u32[]{:S(2)}) collective-permute-start(f32[1,208,384]{2,1,0:T(8,128)} %collective-permute-done.3.refs_3_.refs_5_), channel_id=1, source_target_pairs={{0,8},{8,0},{16,24},{24,16},{1,9},{9,1},{17,25},{25,17},{2,10},{10... | collective-permute-start | bytes 958472 | tf_op jit(solution)/shard_map/ppermute | solution.py:186
  61.4 145.3 %all-gather.4.cloned.1.call-start = ((), (), s32[]{:S(2)}) async-start(), calls=%async_computation.4 | async-start | bytes 7618560 | tf_op jit(solution)/shard_map/all_gather | solution.py:178
  62.2 227.6 %reduce-scatter.11.cloned.1.call-start = ((), (), s32[]{:S(2)}) async-start(), calls=%async_computation.10 | async-start | bytes 3194880 | tf_op jit(solution)/shard_map/reduce_scatter | solution.py:208
  62.2 21.2 %collective-permute-start.6 = (f32[4,208,768]{2,1,0:T(8,128)}, f32[4,208,768]{2,1,0:T(8,128)}, u32[]{:S(2)}, u32[]{:S(2)}) collective-permute-start(f32[4,208,768]{2,1,0:T(8,128)} %product.8.refs_2_), channel_id=1, source_target_pairs={{0,1},{1,0},{2,3},{3,2},{4,5},{5,4},{6,7},{7,6},{8,9},{9,8},{10,11... | collective-permute-start | bytes 7667720 | tf_op jit(solution)/shard_map/ppermute | solution.py:203
  87.7 204.1 %reduce-scatter.9.cloned.1.call-start = ((), (), s32[]{:S(2)}) async-start(), calls=%async_computation.9 | async-start | bytes 4177920 | tf_op jit(solution)/shard_map/reduce_scatter | solution.py:208
  111.3 23.7 %collective-permute-start.7 = (f32[4,272,768]{2,1,0:T(8,128)}, f32[4,272,768]{2,1,0:T(8,128)}, u32[]{:S(2)}, u32[]{:S(2)}) collective-permute-start(f32[4,272,768]{2,1,0:T(8,128)} %product.10.refs_2_), channel_id=1, source_target_pairs={{0,1},{1,0},{2,3},{3,2},{4,5},{5,4},{6,7},{7,6},{8,9},{9,8},{10,11... | collective-permute-start | bytes 10027016 | tf_op jit(solution)/shard_map/ppermute | solution.py:203
  140.2 153.6 %reduce-scatter.7.cloned.1.call-start = ((), (), s32[]{:S(2)}) async-start(), calls=%async_computation.8 | async-start | bytes 5652480 | tf_op jit(solution)/shard_map/reduce_scatter | solution.py:208
  170.8 29.3 %collective-permute-start.8 = (f32[4,368,768]{2,1,0:T(8,128)}, f32[4,368,768]{2,1,0:T(8,128)}, u32[]{:S(2)}, u32[]{:S(2)}) collective-permute-start(f32[4,368,768]{2,1,0:T(8,128)} %product.12.refs_2_), channel_id=1, source_target_pairs={{0,1},{1,0},{2,3},{3,2},{4,5},{5,4},{6,7},{7,6},{8,9},{9,8},{10,11... | collective-permute-start | bytes 13565960 | tf_op jit(solution)/shard_map/ppermute | solution.py:203
  206.5 193.7 %reduce-scatter.5.cloned.1.call-start = ((), (), s32[]{:S(2)}) async-start(), calls=%async_computation.7 | async-start | bytes 7618560 | tf_op jit(solution)/shard_map/reduce_scatter | solution.py:208
  244.0 37.8 %collective-permute-start.9 = (f32[4,496,768]{2,1,0:T(8,128)}, f32[4,496,768]{2,1,0:T(8,128)}, u32[]{:S(2)}, u32[]{:S(2)}) collective-permute-start(f32[4,496,768]{2,1,0:T(8,128)} %product.14.refs_2_), channel_id=1, source_target_pairs={{0,1},{1,0},{2,3},{3,2},{4,5},{5,4},{6,7},{7,6},{8,9},{9,8},{10,11... | collective-permute-start | bytes 18284552 | tf_op jit(solution)/shard_map/ppermute | solution.py:203
Sparse Core Ops, SparseCore 0:
  31.8 45.8 all-gather.7
  79.6 55.4 all-gather.5
  137.0 68.5 all-gather.3
Sparse Core Ops, SparseCore 1:
  87.7 52.4 reduce-scatter.10
  142.5 62.8 reduce-scatter.8
  207.6 82.1 reduce-scatter.6
  292.2 107.9 reduce-scatter.4

commit v3 on v2

--- a/solution.py
+++ b/solution.py
@@ -7,7 +7,7 @@
 from jax.experimental.pallas import tpu as pltpu
 from jax.sharding import PartitionSpec as P
 
-CUTS = (0.155, 0.36, 0.63)
+CUTS = (0.155, 0.37, 0.643)
 F32, BF16 = jnp.float32, jnp.bfloat16
 LAST = (((1,), (1,)), ((), ()))
 FIRST = (((1,), (0,)), ((), ()))
@@ -200,9 +200,13 @@
     else:
         gather(mixed(range(n)), ())
     for g in range(n):
+        if g == 0:
+            every = run(g, jnp.arange(n_col, dtype=jnp.int32))
+            if square:
+                gather({g: chunks[g] for g in range(2, n)}, ())
+            sums[g] = lax.psum_scatter(every, "col", scatter_dimension=0)
+            continue
         ex = send(run(g, theirs), "col", cores)
-        if g == 0 and square:
-            gather({g: chunks[g] for g in range(2, n)}, ())
         total = run(g, mine) + ex
         token = (total,)
         sums[g] = lax.psum_scatter(total, "col", scatter_dimension=0, axis_index_groups=line)

time: 418 us -> 417 us (level)
  waiting for transfers between devices: 113 us -> 123 us
  Pallas kernels: 248 us -> 241 us
    all_gather x3, waiting for transfers between devices: 0.06 us -> 7.21 us  [gather(): lax.all_gather(chunk, 'row', axis=0 if square else 2, tiled=True)]
    pallas_call x8 -> x7, Pallas kernels: 222 us -> 215 us  [product(): pl.pallas_call(functools.partial(product_kernel, len(parts), len(deps)),...]
    add x4 -> x3, other arithmetic: 23.7 us -> 19.5 us  [per_device(): total = run(g, mine) + ex]
    reduce_scatter x4 -> x3, waiting for transfers between devices: 104 us -> 106 us  [per_device(): lax.psum_scatter(total, 'col', scatter_dimension=0, axis_index_groups=line)]
  transfers between devices with their start and end apart: 17 -> 16, of which waited for: 5 -> 9; matrix products, arithmetic and copies ran while one was open for 6% -> 5% of each run, Pallas kernels for 58% -> 57%
where the time goes in v3:
time: 417 us; the launch traced here: 409 us
  Pallas kernels  241 us (58%)
  waiting for transfers between devices  123 us (29%)
  other arithmetic  20.6 us (5%)
  between operations  15.1 us (4%)
  starting transfers between devices  8.11 us (2%)
    pallas_call x7, Pallas kernels, product(): pl.pallas_call(functools.partial(product_kernel, len(parts), len(deps)),...  215 us
    reduce_scatter x3, waiting for transfers between devices, per_device(): lax.psum_scatter(total, 'col', scatter_dimension=0, axis_index_groups=line)  106 us
    add x3, other arithmetic, per_device(): total = run(g, mine) + ex  19.5 us
    pallas_call x2, Pallas kernels, mix(): pl.pallas_call(functools.partial(mix_kernel, groups, cut), grid=(1,), in_...  17.2 us
    pallas_call x4, Pallas kernels, place(): pl.pallas_call(functools.partial(place_kernel, first), grid=(1,), in_spec...  8.76 us
  transfers between devices with their start and end apart: 16, of which 9 were waited for; matrix products, arithmetic and copies ran while one was open for 5% of the time, Pallas kernels for 57%

profile of v3, /device:TPU:0, one launch (start us, length us, event | category | flops | bytes accessed | tf_op | source)
XLA Modules:
  0.0 408.9 jit_solution(11381141302553290341)
XLA Ops:
  7.4 5.1 %mix.2 = (f32[1,208,384]{2,1,0:T(8,128)}, f32[1,208,384]{2,1,0:T(8,128)}) custom-call(f32[84,84]{1,0:T(8,128)} %coupling_ref.3, f32[84,16,768]{2,1,0:T(8,128)} %bitcast.18), custom_call_target="tpu_custom_call" | custom-call | flops 1288175616 | tf_op jit(solution)/shard_map/mix/pallas_call | solution.py:99
  12.5 3.0 collective-permute-start.2
  15.5 1.5 collective-permute-start
  17.5 12.0 %mix.3 = (f32[1,288,768]{2,1,0:T(8,128)}, f32[1,368,768]{2,1,0:T(8,128)}, f32[1,480,768]{2,1,0:T(8,128)}) custom-call(f32[84,84]{1,0:T(8,128)} %coupling_ref.3, f32[84,16,768]{2,1,0:T(8,128)} %bitcast.19, f32[1,208,384]{2,1,0:T(8,128)} %get-tuple-element.12.refs_0_.refs_1_), custom_call_target="tpu_custom_call" | custom-call | flops 7035420672 | tf_op jit(solution)/shard_map/mix/pallas_call | solution.py:99
  32.2 1.7 collective-permute-start.5
  34.5 5.8 %collective-permute-done.4.refs_6_ = f32[1,208,384]{2,1,0:T(8,128)} collective-permute-done((f32[1,208,384]{2,1,0:T(8,128)}, f32[1,208,384]{2,1,0:T(8,128)}, u32[]{:S(2)}, u32[]{:S(2)}) %collective-permute-start.4) | collective-permute-done | bytes 319520 | tf_op jit(solution)/shard_map/ppermute | solution.py:186
  41.1 35.6 %product.7.refs_2_ = f32[8,208,768]{2,1,0:T(8,128)} custom-call(s32[8]{0:T(128)} %iota.9.where_ref, s32[8]{0:T(128)} %stack.35.at_ref, f32[1,208,384]{2,1,0:T(8,128)} %get-tuple-element.15.refs_0_, f32[1,208,384]{2,1,0:T(8,128)} %get-tuple-element.12.refs_0_.refs_1_, f32[1,208,384]{2,1,0:T(8,128)} %collective-permute-done.refs_2_, ...), custom_call_target="tpu_custom_call" | custom-call | flops 23555211264 | tf_op jit(solution)/shard_map/product/pallas_call | solution.py:60
  79.3 24.1 %product.8.refs_2_ = f32[4,288,768]{2,1,0:T(8,128)} custom-call(s32[4]{0:T(128)} %fusion.where_ref, s32[8]{0:T(128)} %stack.35.at_ref, f32[4,288,768]{2,1,0:T(8,128)} %all-gather.8.cloned.1.call-done.refs_0_, f32[6144,3072]{1,0:T(8,128)} %refs_1_.11, f32[1,368,768]{2,1,0:T(8,128)} %get-tuple-element.18.refs_2_), custom_call_target="tpu_custom_call" | custom-call | flops 16307453952 | tf_op jit(solution)/shard_map/product/pallas_call | solution.py:60
  103.9 24.2 %product.9 = f32[4,288,768]{2,1,0:T(8,128)} custom-call(s32[4]{0:T(128)} %fusion.1.where_ref, s32[8]{0:T(128)} %stack.35.at_ref, f32[4,288,768]{2,1,0:T(8,128)} %all-gather.8.cloned.1.call-done.refs_0_, f32[6144,3072]{1,0:T(8,128)} %refs_1_.11, f32[4,288,768]{2,1,0:T(8,128)} %product.8.refs_2_), custom_call_target="tpu_custom_call" | custom-call | flops 16307453952 | tf_op jit(solution)/shard_map/product/pallas_call | solution.py:60
  128.1 5.3 %add.54.refs_2_ = f32[4,288,768]{2,1,0:T(8,128)} add(f32[4,288,768]{2,1,0:T(8,128)} %product.9, f32[4,288,768]{2,1,0:T(8,128)} %collective-permute-done.6) | non-fusion elementwise | flops 884736 | bytes 10616832 | tf_op jit(solution)/shard_map/add | solution.py:210
  133.7 3.1 all-gather.6.cloned.1.call-done.refs_0_
  136.8 29.2 %product.10.refs_2_ = f32[4,368,768]{2,1,0:T(8,128)} custom-call(s32[4]{0:T(128)} %fusion.where_ref, s32[8]{0:T(128)} %stack.35.at_ref, f32[4,368,768]{2,1,0:T(8,128)} %all-gather.6.cloned.1.call-done.refs_0_, f32[6144,3072]{1,0:T(8,128)} %refs_1_.11, f32[4,288,768]{2,1,0:T(8,128)} %add.54.refs_2_), custom_call_target="tpu_custom_call" | custom-call | flops 20837302272 | tf_op jit(solution)/shard_map/product/pallas_call | solution.py:60
  166.0 29.2 %product.11 = f32[4,368,768]{2,1,0:T(8,128)} custom-call(s32[4]{0:T(128)} %fusion.1.where_ref, s32[8]{0:T(128)} %stack.35.at_ref, f32[4,368,768]{2,1,0:T(8,128)} %all-gather.6.cloned.1.call-done.refs_0_, f32[6144,3072]{1,0:T(8,128)} %refs_1_.11, f32[4,368,768]{2,1,0:T(8,128)} %product.10.refs_2_), custom_call_target="tpu_custom_call" | custom-call | flops 20837302272 | tf_op jit(solution)/shard_map/product/pallas_call | solution.py:60
  195.2 6.4 %add.55.refs_2_ = f32[4,368,768]{2,1,0:T(8,128)} add(f32[4,368,768]{2,1,0:T(8,128)} %product.11, f32[4,368,768]{2,1,0:T(8,128)} %collective-permute-done.7) | non-fusion elementwise | flops 1130496 | bytes 13565952 | tf_op jit(solution)/shard_map/add | solution.py:210
  202.0 3.5 all-gather.4.cloned.1.call-done.refs_0_
  205.6 36.3 %product.12.refs_2_ = f32[4,480,768]{2,1,0:T(8,128)} custom-call(s32[4]{0:T(128)} %fusion.where_ref, s32[8]{0:T(128)} %stack.35.at_ref, f32[4,480,768]{2,1,0:T(8,128)} %all-gather.4.cloned.1.call-done.refs_0_, f32[6144,3072]{1,0:T(8,128)} %refs_1_.11, f32[4,368,768]{2,1,0:T(8,128)} %add.55.refs_2_), custom_call_target="tpu_custom_call" | custom-call | flops 27179089920 | tf_op jit(solution)/shard_map/product/pallas_call | solution.py:60
  241.8 36.5 %product.13 = f32[4,480,768]{2,1,0:T(8,128)} custom-call(s32[4]{0:T(128)} %fusion.1.where_ref, s32[8]{0:T(128)} %stack.35.at_ref, f32[4,480,768]{2,1,0:T(8,128)} %all-gather.4.cloned.1.call-done.refs_0_, f32[6144,3072]{1,0:T(8,128)} %refs_1_.11, f32[4,480,768]{2,1,0:T(8,128)} %product.12.refs_2_), custom_call_target="tpu_custom_call" | custom-call | flops 27179089920 | tf_op jit(solution)/shard_map/product/pallas_call | solution.py:60
  278.3 7.8 %add.56 = f32[4,480,768]{2,1,0:T(8,128)} add(f32[4,480,768]{2,1,0:T(8,128)} %product.13, f32[4,480,768]{2,1,0:T(8,128)} %collective-permute-done.8) | non-fusion elementwise | flops 1474560 | bytes 17694720 | tf_op jit(solution)/shard_map/add | solution.py:210
  286.2 1.9 place.4.refs_0_
  288.1 2.1 place.5.refs_0_
  290.2 1.5 reduce-scatter.7.cloned.1.call-done
  291.7 2.3 place.6.refs_0_
  294.0 104.9 %reduce-scatter.5.cloned.1.call-done = f32[1,480,768]{2,1,0:T(8,128)} async-done(((f32[4,480,768]{2,1,0:T(8,128)}), f32[1,480,768]{2,1,0:T(8,128)}) %reduce-scatter.5.cloned.1.call-update) | async-done | bytes 1474576 | tf_op jit(solution)/shard_map/reduce_scatter | solution.py:212
  398.9 2.5 place.7
  (37 shorter events, 8.4 us)
Async XLA Ops:
  7.4 72.0 %all-gather.8.cloned.1.call-start = ((), (), s32[]{:S(2)}) async-start(), calls=%async_computation.6 | async-start | bytes 4423680 | tf_op jit(solution)/shard_map/all_gather | solution.py:178
  12.5 17.0 %collective-permute-start.2 = (f32[1,208,384]{2,1,0:T(8,128)}, f32[1,208,384]{2,1,0:T(8,128)}, u32[]{:S(2)}, u32[]{:S(2)}) collective-permute-start(f32[1,208,384]{2,1,0:T(8,128)} %get-tuple-element.15.refs_0_), channel_id=1, source_target_pairs={{0,16},{8,24},{16,0},{24,8},{1,17},{9,25},{17,1},{25,9},{2,18},{10... | collective-permute-start | bytes 958472 | tf_op jit(solution)/shard_map/ppermute | solution.py:185
  15.5 14.1 %collective-permute-start = (f32[1,208,384]{2,1,0:T(8,128)}, f32[1,208,384]{2,1,0:T(8,128)}, u32[]{:S(2)}, u32[]{:S(2)}) collective-permute-start(f32[1,208,384]{2,1,0:T(8,128)} %get-tuple-element.15.refs_0_), channel_id=1, source_target_pairs={{0,8},{8,0},{16,24},{24,16},{1,9},{9,1},{17,25},{25,17},{2,10},{10... | collective-permute-start | bytes 958472 | tf_op jit(solution)/shard_map/ppermute | solution.py:184
  16.9 13.2 %collective-permute-start.3 = (f32[1,208,384]{2,1,0:T(8,128)}, f32[1,208,384]{2,1,0:T(8,128)}, u32[]{:S(2)}, u32[]{:S(2)}) collective-permute-start(f32[1,208,384]{2,1,0:T(8,128)} %get-tuple-element.12.refs_0_.refs_1_), channel_id=1, source_target_pairs={{0,16},{8,24},{16,0},{24,8},{1,17},{9,25},{17,1},{25,9},{2,18},{10... | collective-permute-start | bytes 958472 | tf_op jit(solution)/shard_map/ppermute | solution.py:184
  17.5 14.2 %collective-permute-start.1 = (f32[1,208,384]{2,1,0:T(8,128)}, f32[1,208,384]{2,1,0:T(8,128)}, u32[]{:S(2)}, u32[]{:S(2)}) collective-permute-start(f32[1,208,384]{2,1,0:T(8,128)} %get-tuple-element.12.refs_0_.refs_1_), channel_id=1, source_target_pairs={{0,8},{8,0},{16,24},{24,16},{1,9},{9,1},{17,25},{25,17},{2,10},{10... | collective-permute-start | bytes 958472 | tf_op jit(solution)/shard_map/ppermute | solution.py:185
  31.6 105.2 %all-gather.6.cloned.1.call-start = ((), (), s32[]{:S(2)}) async-start(), calls=%async_computation.5 | async-start | bytes 5652480 | tf_op jit(solution)/shard_map/all_gather | solution.py:178
  31.9 8.5 %collective-permute-start.4 = (f32[1,208,384]{2,1,0:T(8,128)}, f32[1,208,384]{2,1,0:T(8,128)}, u32[]{:S(2)}, u32[]{:S(2)}) collective-permute-start(f32[1,208,384]{2,1,0:T(8,128)} %collective-permute-done.refs_2_), channel_id=1, source_target_pairs={{0,16},{8,24},{16,0},{24,8},{1,17},{9,25},{17,1},{25,9},{2,18},{10... | collective-permute-start | bytes 958472 | tf_op jit(solution)/shard_map/ppermute | solution.py:186
  32.2 8.4 %collective-permute-start.5 = (f32[1,208,384]{2,1,0:T(8,128)}, f32[1,208,384]{2,1,0:T(8,128)}, u32[]{:S(2)}, u32[]{:S(2)}) collective-permute-start(f32[1,208,384]{2,1,0:T(8,128)} %collective-permute-done.3.refs_3_.refs_5_), channel_id=1, source_target_pairs={{0,8},{8,0},{16,24},{24,16},{1,9},{9,1},{17,25},{25,17},{2,10},{10... | collective-permute-start | bytes 958472 | tf_op jit(solution)/shard_map/ppermute | solution.py:186
  76.8 128.8 %all-gather.4.cloned.1.call-start = ((), (), s32[]{:S(2)}) async-start(), calls=%async_computation.4 | async-start | bytes 7372800 | tf_op jit(solution)/shard_map/all_gather | solution.py:178
  77.5 208.6 %reduce-scatter.11.cloned.1.call-start = ((), (), s32[]{:S(2)}) async-start(), calls=%async_computation.10 | async-start | bytes 5750784 | tf_op jit(solution)/shard_map/reduce_scatter | solution.py:207
  78.1 210.0 %reduce-scatter.9.cloned.1.call-start = ((), (), s32[]{:S(2)}) async-start(), calls=%async_computation.9 | async-start | bytes 4423680 | tf_op jit(solution)/shard_map/reduce_scatter | solution.py:212
  103.4 24.7 %collective-permute-start.6 = (f32[4,288,768]{2,1,0:T(8,128)}, f32[4,288,768]{2,1,0:T(8,128)}, u32[]{:S(2)}, u32[]{:S(2)}) collective-permute-start(f32[4,288,768]{2,1,0:T(8,128)} %product.8.refs_2_), channel_id=1, source_target_pairs={{0,1},{1,0},{2,3},{3,2},{4,5},{5,4},{6,7},{7,6},{8,9},{9,8},{10,11... | collective-permute-start | bytes 10616840 | tf_op jit(solution)/shard_map/ppermute | solution.py:209
  133.4 158.2 %reduce-scatter.7.cloned.1.call-start = ((), (), s32[]{:S(2)}) async-start(), calls=%async_computation.8 | async-start | bytes 5652480 | tf_op jit(solution)/shard_map/reduce_scatter | solution.py:212
  166.0 29.2 %collective-permute-start.7 = (f32[4,368,768]{2,1,0:T(8,128)}, f32[4,368,768]{2,1,0:T(8,128)}, u32[]{:S(2)}, u32[]{:S(2)}) collective-permute-start(f32[4,368,768]{2,1,0:T(8,128)} %product.10.refs_2_), channel_id=1, source_target_pairs={{0,1},{1,0},{2,3},{3,2},{4,5},{5,4},{6,7},{7,6},{8,9},{9,8},{10,11... | collective-permute-start | bytes 13565960 | tf_op jit(solution)/shard_map/ppermute | solution.py:209
  201.6 197.3 %reduce-scatter.5.cloned.1.call-start = ((), (), s32[]{:S(2)}) async-start(), calls=%async_computation.7 | async-start | bytes 7372800 | tf_op jit(solution)/shard_map/reduce_scatter | solution.py:212
  241.8 36.5 %collective-permute-start.8 = (f32[4,480,768]{2,1,0:T(8,128)}, f32[4,480,768]{2,1,0:T(8,128)}, u32[]{:S(2)}, u32[]{:S(2)}) collective-permute-start(f32[4,480,768]{2,1,0:T(8,128)} %product.12.refs_2_), channel_id=1, source_target_pairs={{0,1},{1,0},{2,3},{3,2},{4,5},{5,4},{6,7},{7,6},{8,9},{9,8},{10,11... | collective-permute-start | bytes 17694728 | tf_op jit(solution)/shard_map/ppermute | solution.py:209
Sparse Core Ops, SparseCore 0:
  31.8 47.5 all-gather.7
  81.3 55.4 all-gather.5
  138.6 66.8 all-gather.3
Sparse Core Ops, SparseCore 1:
  80.3 59.7 reduce-scatter.10
  142.4 64.8 reduce-scatter.8
  209.5 82.1 reduce-scatter.6
  294.0 104.8 reduce-scatter.4
